TPU v7x, 32 devices: a whole 2x2x4 slice. The times are simulated.
32 devices in a mesh: gx: 8 (over y, x, core), gy: 4 (over z).
Axes of the slice: x: 2, y: 2, z: 4, core: 2. Of those that a mesh axis runs over, the one named last changes fastest.
Arguments:
- velocity: float32 [3, 128, 64, 512], P(None, 'gx', 'gy'), may hold values from -6 to 6
- stress: float32 [6, 128, 64, 512], P(None, 'gx', 'gy'), may hold values from -6 to 6
- pier_velocity: float32 [128, 16], P('gx', 'gy'), may hold values from -6 to 6
- buoyancy: float32 [128, 64, 512], P('gx', 'gy'), may hold values from 0.5 to 2
- layer: int32 [128], P('gx'), may hold values from 0 to 7, as said below
- lame_table: float32 [8], replicated, may hold values from 0.3 to 1.2
- shear_table: float32 [8], replicated, may hold values from 0.2 to 0.8
- relax_table: float32 [8], replicated, may hold values from 0.6 to 0.95
- impedance: float32 [16], P('gy'), may hold values from 0.5 to 2
- footprint: int32 [16, 16], replicated, may hold values from 0 to 32767, as said below
- damp_inverse: float32 [128, 128], replicated
Outputs:
- velocity_out: float32 [3, 128, 64, 512], P(None, 'gx', 'gy')
- stress_out: float32 [6, 128, 64, 512], P(None, 'gx', 'gy')
- pier_out: float32 [128, 16], P('gx', 'gy')
Inputs may be any that keep to these rules, and one draw needn't show every extreme that they name: `footprint`: row p lists the 16 cells of a square of 4 by 4 cells, row by row; squares may intersect and lie anywhere in the plane. `layer`: non-decreasing along depth; the first cell is in layer 0 and the last in layer 7.
All inputs are finite; a program needn't handle non-finite values.
Results may differ from a plain program's by a relative error of at most 0.00011.
Values sent between devices are 32-bit elements; how exact they have to be, the bound alone decides.
A program may use at most 192 MiB of HBM per device.

v0:
```python
import jax
import jax.numpy as jnp
from jax import lax
from jax.sharding import PartitionSpec as P

STEPS = 2
FOOT = 16
grid_ratio = 0.25
soil_gain = 0.2
pier_gain = 0.5


def extended(cells, sides, width):
    for axis, dim in sides:
        count = lax.axis_size(axis)
        ends = count - 1
        head = lax.slice_in_dim(cells, 0, width, axis=dim)
        tail = lax.slice_in_dim(cells, cells.shape[dim] - width, cells.shape[dim], axis=dim)
        cells = jnp.concatenate(
            [
                lax.ppermute(tail, axis, [(i, (i + 1) % count) for i in range(ends)]),
                cells,
                lax.ppermute(head, axis, [((i + 1) % count, i) for i in range(ends)]),
            ],
            axis=dim,
        )
    return cells


def forward_diff(padded, along):
    center = padded[1:-1, 1:-1, 1:-1]
    if along == 0:
        return padded[2:, 1:-1, 1:-1] - center
    if along == 1:
        return padded[1:-1, 2:, 1:-1] - center
    return padded[1:-1, 1:-1, 2:] - center


def backward_diff(padded, along):
    center = padded[1:-1, 1:-1, 1:-1]
    if along == 0:
        return center - padded[:-2, 1:-1, 1:-1]
    if along == 1:
        return center - padded[1:-1, :-2, 1:-1]
    return center - padded[1:-1, 1:-1, :-2]


def move_velocity(velocity, padded, buoyancy):
    scaled = grid_ratio * buoyancy
    first = velocity[0] + scaled * (
        backward_diff(padded[0], 2) + forward_diff(padded[3], 1) + forward_diff(padded[4], 0)
    )
    second = velocity[1] + scaled * (
        forward_diff(padded[3], 2) + backward_diff(padded[1], 1) + forward_diff(padded[5], 0)
    )
    third = velocity[2] + scaled * (
        forward_diff(padded[4], 2) + forward_diff(padded[5], 1) + backward_diff(padded[2], 0)
    )
    return jnp.stack([first, second, third])


def move_stress(stress, padded, lame_first, shear_mod, relax):
    strain_x = forward_diff(padded[0], 2)
    strain_y = forward_diff(padded[1], 1)
    strain_z = forward_diff(padded[2], 0)
    modulus = lame_first + 2.0 * shear_mod
    normal_x = relax * stress[0] + grid_ratio * (
        modulus * strain_x + lame_first * (strain_y + strain_z)
    )
    normal_y = relax * stress[1] + grid_ratio * (
        modulus * strain_y + lame_first * (strain_x + strain_z)
    )
    normal_z = relax * stress[2] + grid_ratio * (
        modulus * strain_z + lame_first * (strain_x + strain_y)
    )
    shear_xy = relax * stress[3] + grid_ratio * shear_mod * (
        backward_diff(padded[0], 1) + backward_diff(padded[1], 2)
    )
    shear_xz = relax * stress[4] + grid_ratio * shear_mod * (
        backward_diff(padded[0], 0) + backward_diff(padded[2], 2)
    )
    shear_yz = relax * stress[5] + grid_ratio * shear_mod * (
        backward_diff(padded[1], 0) + backward_diff(padded[2], 1)
    )
    return jnp.stack([normal_x, normal_y, normal_z, shear_xy, shear_xz, shear_yz])


def layer_values(layer, table):
    levels = jnp.arange(table.shape[0], dtype=jnp.int32)
    onehot = (layer[:, None] == levels[None, :]).astype(table.dtype)
    return jnp.sum(onehot * table[None, :], axis=1)[:, None, None]


def with_faces(fields):
    padded = extended(fields, (("gx", 1), ("gy", 2)), 1)
    return jnp.pad(padded, ((0, 0), (0, 0), (0, 0), (1, 1)))


def footprint_matches(cell_ids, footprint):
    piers = footprint.shape[0]
    equal = (cell_ids[:, None] == footprint.reshape(-1)[None, :]).astype(jnp.float32)
    return jnp.sum(equal.reshape(cell_ids.shape[0], piers, FOOT), axis=2)


def damp_columns(velocity, inverse):
    pencils = lax.all_to_all(velocity, "gx", split_axis=3, concat_axis=1, tiled=True)
    shape = pencils.shape
    flat = pencils.reshape(shape[0], shape[1], shape[2] * shape[3])
    damped = jnp.einsum("zk,fkm->fzm", inverse, flat, precision=lax.Precision.HIGHEST).reshape(
        shape
    )
    return lax.all_to_all(damped, "gx", split_axis=1, concat_axis=3, tiled=True)


def body(
    velocity,
    stress,
    pier_velocity,
    buoyancy,
    layer,
    lame_table,
    shear_table,
    relax_table,
    impedance,
    footprint,
    damp_inverse,
):
    depth_cells, side_cells, line_cells = (velocity.shape[1], velocity.shape[2], velocity.shape[3])
    own_piers = pier_velocity.shape[1]
    lame_first = layer_values(layer, lame_table)
    shear_mod = layer_values(layer, shear_table)
    relax = layer_values(layer, relax_table)
    row_start = lax.axis_index("gy") * side_cells
    cell_ids = row_start * line_cells + jnp.arange(side_cells * line_cells, dtype=jnp.int32)
    selector = footprint_matches(cell_ids, footprint)
    own_foot = lax.dynamic_slice_in_dim(footprint, lax.axis_index("gy") * own_piers, own_piers, 0)
    for time_step in range(STEPS):
        padded = with_faces(stress)
        velocity = move_velocity(velocity, padded, buoyancy)
        vertical = velocity[2].reshape(depth_cells, side_cells * line_cells)
        piece = lax.all_gather(velocity[2], "gy", axis=1, tiled=True)
        count = piece.shape[1]
        piece_ids = jnp.arange(count * line_cells, dtype=jnp.int32)
        picks = footprint_matches(piece_ids, own_foot)
        flat = piece.reshape(depth_cells, count * line_cells)
        summed = jnp.dot(
            flat, picks, precision=lax.Precision.HIGHEST, preferred_element_type=jnp.float32
        )
        mean_speed = summed / FOOT
        force = impedance[None, :] * (pier_velocity - mean_speed)
        pier_velocity = pier_velocity - pier_gain * force
        all_force = lax.all_gather(force, "gy", axis=1, tiled=True)
        pushed = jnp.dot(
            all_force,
            selector.T,
            precision=lax.Precision.HIGHEST,
            preferred_element_type=jnp.float32,
        )
        vertical = vertical + soil_gain * pushed
        velocity = jnp.stack(
            [velocity[0], velocity[1], vertical.reshape(depth_cells, side_cells, line_cells)]
        )
        velocity = damp_columns(velocity, damp_inverse)
        padded = with_faces(velocity)
        stress = move_stress(stress, padded, lame_first, shear_mod, relax)
    return (velocity, stress, pier_velocity)


def solution(mesh):
    placed = (
        P(None, "gx", "gy", None),
        P(None, "gx", "gy", None),
        P("gx", "gy"),
        P("gx", "gy", None),
        P("gx"),
        P(),
        P(),
        P(),
        P("gy"),
        P(),
        P(),
    )
    return jax.shard_map(
        body,
        mesh=mesh,
        in_specs=placed,
        out_specs=(P(None, "gx", "gy", None), P(None, "gx", "gy", None), P("gx", "gy")),
        check_vma=False,
    )
```

profile of v0, /device:TPU:11, one launch (start us, length us, event | category | flops | bytes accessed | tf_op | source)
XLA Modules:
  0.0 499.5 jit_solution(11973510932062096920)
XLA Ops:
  8.3 3.7 collective-permute-start
  16.9 3.0 collective-permute-done.1
  20.3 3.2 collective-permute-start.2
  28.5 3.2 collective-permute-done.3
  31.7 4.2 select_maximum_fusion.4
  47.9 5.0 fusion.58
  52.8 31.2 %all-gather.5.cloned.1.call-done = f32[16,64,512]{2,1,0:T(8,128)} async-done(((f32[16,16,512]{2,1,0:T(8,128)}), f32[16,64,512]{2,1,0:T(8,128)}) %all-gather.5.cloned.1.call-update) | async-done | bytes 2097168 | tf_op jit(solution)/shard_map/all_gather | solution.py:141
  89.5 9.2 %all-gather = f32[4,4,16]{2,1,0:T(4,128)S(1)} all-gather(f32[1,4,16]{2,1,0:T(4,128)S(1)} %bitcast.214), channel_id=1, replica_groups=mesh['gx'=8,'gy'=4] {'gy'}, dimensions={0}, use_global_device_ids=true | all-gather | bytes 1280 | tf_op jit(solution)/shard_map/all_gather | solution.py:152
  99.9 8.8 %copy.50 = f32[3,16,16,512]{2,1,0,3:T(8,128)} copy(f32[3,16,16,512]{3,2,1,0:T(8,128)S(1)} %pad_maximum_fusion) | data formatting | bytes 3145728 | tf_op jit(solution)/shard_map/stack | solution.py:160
  108.7 8.9 %reshape.89 = f32[8,1,49152]{2,1,0:T(1,128)S(1)} reshape(f32[512,3,16,16]{3,2,1,0:T(8,128)} %bitcast.186) | data formatting | bytes 3145728
  117.5 26.2 %all_to_all.66 = f32[8,1,49152]{2,1,0:T(1,128)S(1)} all-to-all(f32[8,1,49152]{2,1,0:T(1,128)S(1)} %reshape.89), channel_id=1, replica_groups=mesh['gx'=8,'gy'=4] {'gx'}, dimensions={0} | all-to-all | bytes 3145728 | tf_op jit(solution)/shard_map/all_to_all | solution.py:106
  144.3 4.4 reduce
  148.8 8.7 %reshape.90 = f32[512,3,16,16]{3,2,1,0:T(8,128)} reshape(f32[8,49152]{1,0:T(8,128)S(1)} %reduce) | data formatting | bytes 3145728
  157.5 8.1 %copy.51 = f32[3,16,16,8,64]{4,2,1,3,0:T(8,128)S(1)} copy(f32[3,16,16,8,64]{2,1,0,4,3:T(8,128)} %bitcast.188) | data formatting | bytes 3145728 | tf_op jit(solution)/shard_map/all_to_all | solution.py:106
  167.4 5.2 %fusion.65 = f32[3,1024,128]{2,1,0:T(8,128)} fusion(f32[3,128,1024]{2,1,0:T(8,128)} %reshape.79, f32[128,128]{1,0:T(8,128)S(1)} %copy-done), kind=kOutput, calls=%fused_computation.160 | convolution fusion | flops 603979776 | bytes 3211264 | tf_op jit(solution)/shard_map/zk,fkm->fzm/dot_general | solution.py:109
  175.2 3.0 reshape.91
  178.2 24.5 %all_to_all.67 = f32[8,1,49152]{2,1,0:T(1,128)S(1)} all-to-all(f32[8,1,49152]{2,1,0:T(1,128)} %reshape.91), channel_id=1, replica_groups=mesh['gx'=8,'gy'=4] {'gx'}, dimensions={0} | all-to-all | bytes 3145728 | tf_op jit(solution)/shard_map/all_to_all | solution.py:112
  202.7 6.2 %reduce.1 = f32[8,49152]{1,0:T(8,128)} reduce(f32[8,1,49152]{2,1,0:T(1,128)S(1)} %all_to_all.67, f32[]{:T(128)} %broadcast.158), dimensions={1}, to_apply=%all_to_all.51.reduce_sub_computation | reduce | bytes 3145732 | tf_op jit(solution)/shard_map/all_to_all | solution.py:112
  211.5 3.5 copy.56
  215.0 3.8 all_to_all.54
  219.8 3.6 collective-permute-start.4
  227.0 3.3 collective-permute-done.5
  230.5 3.8 collective-permute-start.6
  236.4 3.4 collective-permute-done.7
  253.2 3.2 collective-permute-start.8
  259.1 5.3 %collective-permute-done.9 = f32[6,1,16,512]{3,2,1,0:T(8,128)S(1)} collective-permute-done((f32[6,1,16,512]{3,2,1,0:T(8,128)S(1)}, f32[6,1,16,512]{3,2,1,0:T(8,128)S(1)}, u32[]{:S(2)}, u32[]{:S(2)}) %collective-permute-start.9) | collective-permute-done | bytes 196640 | tf_op jit(solution)/shard_map/ppermute | solution.py:23
  267.5 4.2 collective-permute-start.11
  277.3 5.8 %select_maximum_fusion = f32[6,18,18,514]{3,2,1,0:T(8,128)S(1)} fusion(f32[6,18,1,512]{3,2,1,0:T(1,128)} %collective-permute-done.11, f32[6,18,1,512]{3,2,1,0:T(1,128)} %collective-permute-done.10, f32[6,1,16,512]{3,2,1,0:T(8,128)} %copy-done.25, f32[6,16,16,512]{3,2,1,0:T(8,128)S(1)} %copy-done.2, f32[6,1,16,512]{3,2,1,0:T(8,128)S(1)} %collective-permute-done.8), kind=kLoop, calls=%fused_computation.9 | loop fusion | flops 11990592 | bytes 7978176 | tf_op jit(solution)/shard_map/concatenate | solution.py:19
  291.8 3.0 copy.57
  298.2 5.7 %fusion.35 = (f32[1,16,16,512]{3,2,1,0:T(8,128)S(1)}, f32[1,16,16,512]{3,2,1,0:T(8,128)}) fusion(f32[16,16,512]{2,1,0:T(8,128)} %squeeze.117, f32[18,18,514]{2,1,0:T(8,128)S(1)} %get-tuple-element.21, f32[18,18,514]{2,1,0:T(8,128)} %get-tuple-element.22, f32[18,18,514]{2,1,0:T(8,128)} %get-tuple-element.18, f32[16,16,512]{2,1,0:T(8,128)S(1)} %copy-done.5, ...), kind=kLoop, calls=%fused_computation.92 | loop fusion | flops 1966080 | bytes 8388608 | tf_op jit(solution)/shard_map/stack | solution.py:59
  303.9 24.7 %all-gather.7.cloned.1.call-done = f32[16,64,512]{2,1,0:T(8,128)} async-done(((f32[16,16,512]{2,1,0:T(8,128)}), f32[16,64,512]{2,1,0:T(8,128)}) %all-gather.7.cloned.1.call-update) | async-done | bytes 2097168 | tf_op jit(solution)/shard_map/all_gather | solution.py:141
  331.5 3.2 multiply_subtract_fusion
  334.7 9.2 %all-gather.1 = f32[4,4,16]{2,1,0:T(4,128)S(1)} all-gather(f32[1,4,16]{2,1,0:T(4,128)S(1)} %bitcast.215), channel_id=1, replica_groups=mesh['gx'=8,'gy'=4] {'gy'}, dimensions={0}, use_global_device_ids=true | all-gather | bytes 1280 | tf_op jit(solution)/shard_map/all_gather | solution.py:152
  345.1 8.8 %copy.59 = f32[3,16,16,512]{2,1,0,3:T(8,128)} copy(f32[3,16,16,512]{3,2,1,0:T(8,128)S(1)} %pad_maximum_fusion.1) | data formatting | bytes 3145728 | tf_op jit(solution)/shard_map/stack | solution.py:160
  353.9 8.9 %reshape.93 = f32[8,1,49152]{2,1,0:T(1,128)S(1)} reshape(f32[512,3,16,16]{3,2,1,0:T(8,128)} %bitcast.187) | data formatting | bytes 3145728
  362.7 26.4 %all_to_all.68 = f32[8,1,49152]{2,1,0:T(1,128)S(1)} all-to-all(f32[8,1,49152]{2,1,0:T(1,128)S(1)} %reshape.93), channel_id=1, replica_groups=mesh['gx'=8,'gy'=4] {'gx'}, dimensions={0} | all-to-all | bytes 3145728 | tf_op jit(solution)/shard_map/all_to_all | solution.py:106
  389.2 4.4 reduce.2
  393.6 8.7 %reshape.94 = f32[512,3,16,16]{3,2,1,0:T(8,128)} reshape(f32[8,49152]{1,0:T(8,128)S(1)} %reduce.2) | data formatting | bytes 3145728
  402.3 8.1 %copy.60 = f32[3,16,16,8,64]{4,2,1,3,0:T(8,128)S(1)} copy(f32[3,16,16,8,64]{2,1,0,4,3:T(8,128)} %bitcast.189) | data formatting | bytes 3145728 | tf_op jit(solution)/shard_map/all_to_all | solution.py:106
  412.2 5.2 %fusion.63 = f32[3,1024,128]{2,1,0:T(8,128)} fusion(f32[3,128,1024]{2,1,0:T(8,128)} %reshape.82, f32[128,128]{1,0:T(8,128)S(1)} %copy-done), kind=kOutput, calls=%fused_computation.158 | convolution fusion | flops 603979776 | bytes 3211264 | tf_op jit(solution)/shard_map/zk,fkm->fzm/dot_general | solution.py:109
  419.8 3.0 reshape.95
  422.8 24.5 %all_to_all.69 = f32[8,1,49152]{2,1,0:T(1,128)S(1)} all-to-all(f32[8,1,49152]{2,1,0:T(1,128)} %reshape.95), channel_id=1, replica_groups=mesh['gx'=8,'gy'=4] {'gx'}, dimensions={0} | all-to-all | bytes 3145728 | tf_op jit(solution)/shard_map/all_to_all | solution.py:112
  447.3 6.2 %reduce.3 = f32[8,49152]{1,0:T(8,128)} reduce(f32[8,1,49152]{2,1,0:T(1,128)S(1)} %all_to_all.69, f32[]{:T(128)} %broadcast.158), dimensions={1}, to_apply=%all_to_all.58.reduce_sub_computation | reduce | bytes 3145732 | tf_op jit(solution)/shard_map/all_to_all | solution.py:112
  456.1 3.5 copy.64
  462.5 3.6 collective-permute-start.12
  468.2 4.7 collective-permute-done.13
  473.1 3.8 collective-permute-start.14
  479.1 3.3 collective-permute-done.15
  (158 shorter events, 109.4 us)
Async XLA Ops:
  7.2 160.2 %copy-start = (f32[128,128]{1,0:T(8,128)S(1)}, f32[128,128]{1,0:T(8,128)}, u32[]{:S(2)}) copy-start(f32[128,128]{1,0:T(8,128)} %param.21) | copy-start | bytes 196612
  7.2 76.8 %all-gather.5.cloned.1.call-start = ((), (), s32[]{:S(2)}) async-start(), calls=%async_computation.4 | async-start | bytes 2621440 | tf_op jit(solution)/shard_map/all_gather | solution.py:141
  8.3 6.3 %collective-permute-start = (f32[6,1,16,512]{3,2,1,0:T(8,128)S(1)}, f32[6,1,16,512]{3,2,1,0:T(8,128)S(1)}, u32[]{:S(2)}, u32[]{:S(2)}) collective-permute-start(f32[6,1,16,512]{3,2,1,0:T(8,128)S(1)} %get-tuple-element.48), channel_id=1, source_target_pairs={{0,4},{4,8},{8,12},{12,16},{16,20},{20,24},{24,28},{1,5},{5,9},{9,... | collective-permute-start | bytes 589832 | tf_op jit(solution)/shard_map/ppermute | solution.py:21
  12.0 7.9 %collective-permute-start.1 = (f32[6,1,16,512]{3,2,1,0:T(8,128)S(1)}, f32[6,1,16,512]{3,2,1,0:T(8,128)S(1)}, u32[]{:S(2)}, u32[]{:S(2)}) collective-permute-start(f32[6,1,16,512]{3,2,1,0:T(8,128)S(1)} %get-tuple-element.47), channel_id=1, source_target_pairs={{4,0},{8,4},{12,8},{16,12},{20,16},{24,20},{28,24},{5,1},{9,5},{13... | collective-permute-start | bytes 589832 | tf_op jit(solution)/shard_map/ppermute | solution.py:23
  20.3 8.2 %collective-permute-start.2 = (f32[6,18,1,512]{3,2,1,0:T(1,128)S(1)}, f32[6,18,1,512]{3,2,1,0:T(1,128)S(1)}, u32[]{:S(2)}, u32[]{:S(2)}) collective-permute-start(f32[6,18,1,512]{3,2,1,0:T(1,128)S(1)} %get-tuple-element.32), channel_id=1, source_target_pairs={{0,1},{1,2},{2,3},{4,5},{5,6},{6,7},{8,9},{9,10},{10,11},{12,13},{... | collective-permute-start | bytes 663560 | tf_op jit(solution)/shard_map/ppermute | solution.py:21
  23.5 8.2 %collective-permute-start.3 = (f32[6,18,1,512]{3,2,1,0:T(1,128)S(1)}, f32[6,18,1,512]{3,2,1,0:T(1,128)S(1)}, u32[]{:S(2)}, u32[]{:S(2)}) collective-permute-start(f32[6,18,1,512]{3,2,1,0:T(1,128)S(1)} %get-tuple-element.33), channel_id=1, source_target_pairs={{1,0},{2,1},{3,2},{5,4},{6,5},{7,6},{9,8},{10,9},{11,10},{13,12},{... | collective-permute-start | bytes 663560 | tf_op jit(solution)/shard_map/ppermute | solution.py:23
  35.9 1.8 copy-start.4
  37.8 3.1 copy-start.27
  40.6 288.0 %all-gather.7.cloned.1.call-start = ((), (), s32[]{:S(2)}) async-start(), calls=%async_computation.5 | async-start | bytes 2621440 | tf_op jit(solution)/shard_map/all_gather | solution.py:141
  40.8 7.0 %copy-start.7 = (f32[18,18,514]{2,1,0:T(8,128)S(1)}, f32[18,18,514]{2,1,0:T(8,128)}, u32[]{:S(2)}) copy-start(f32[18,18,514]{2,1,0:T(8,128)} %get-tuple-element.28) | copy-start | bytes 1998436
  45.5 53.2 %copy-start.8 = (f32[8192,16]{0,1:T(8,128)}, f32[8192,16]{0,1:T(8,128)S(1)}, u32[]{:S(2)}) copy-start(f32[8192,16]{0,1:T(8,128)S(1)} %convert_reduce_fusion) | copy-start | bytes 1572868
  84.0 2.9 copy-start.11
  84.0 2.9 copy-start.28
  84.0 2.9 copy-start.29
  86.9 11.9 %copy-start.15 = (f32[2,8,16,512]{3,1,2,0:T(8,128)S(1)}, f32[2,8,16,512]{3,1,2,0:T(8,128)}, u32[]{:S(2)}) copy-start(f32[2,8,16,512]{3,1,2,0:T(8,128)} %copy.69) | copy-start | bytes 1572868
  86.9 12.8 %copy-start.17 = (f32[1,16,16,512]{3,2,1,0:T(8,128)S(1)}, f32[1,16,16,512]{3,2,1,0:T(8,128)}, u32[]{:S(2)}) copy-start(f32[1,16,16,512]{3,2,1,0:T(8,128)} %get-tuple-element.40) | copy-start | bytes 1572868
  86.9 12.8 %copy-start.18 = (f32[1,16,16,512]{3,2,1,0:T(8,128)S(1)}, f32[1,16,16,512]{3,2,1,0:T(8,128)}, u32[]{:S(2)}) copy-start(f32[1,16,16,512]{3,2,1,0:T(8,128)} %get-tuple-element.41) | copy-start | bytes 1572868
  215.0 8.3 %copy-start.30 = (f32[8]{0:T(128)S(1)}, f32[8]{0:T(128)}, u32[]{:S(2)}) copy-start(f32[8]{0:T(128)} %param.18) | copy-start | bytes 100
  215.0 8.3 %copy-start.31 = (s32[16]{0:T(128)S(1)}, s32[16]{0:T(128)}, u32[]{:S(2)}) copy-start(s32[16]{0:T(128)} %param.15) | copy-start | bytes 196
  215.0 8.3 %copy-start.32 = (f32[8]{0:T(128)S(1)}, f32[8]{0:T(128)}, u32[]{:S(2)}) copy-start(f32[8]{0:T(128)} %param.17) | copy-start | bytes 100
  215.0 8.3 %copy-start.33 = (f32[8]{0:T(128)S(1)}, f32[8]{0:T(128)}, u32[]{:S(2)}) copy-start(f32[8]{0:T(128)} %param.16) | copy-start | bytes 100
  219.8 5.6 %collective-permute-start.4 = (f32[3,1,16,512]{3,2,1,0:T(8,128)S(1)}, f32[3,1,16,512]{3,2,1,0:T(8,128)S(1)}, u32[]{:S(2)}, u32[]{:S(2)}) collective-permute-start(f32[3,1,16,512]{3,2,1,0:T(8,128)S(1)} %get-tuple-element.58), channel_id=1, source_target_pairs={{0,4},{4,8},{8,12},{12,16},{16,20},{20,24},{24,28},{1,5},{5,9},{9,... | collective-permute-start | bytes 294920 | tf_op jit(solution)/shard_map/ppermute | solution.py:21
  223.5 6.8 %collective-permute-start.5 = (f32[3,1,16,512]{3,2,1,0:T(8,128)S(1)}, f32[3,1,16,512]{3,2,1,0:T(8,128)S(1)}, u32[]{:S(2)}, u32[]{:S(2)}) collective-permute-start(f32[3,1,16,512]{3,2,1,0:T(8,128)S(1)} %get-tuple-element.57), channel_id=1, source_target_pairs={{4,0},{8,4},{12,8},{16,12},{20,16},{24,20},{28,24},{5,1},{9,5},{13... | collective-permute-start | bytes 294920 | tf_op jit(solution)/shard_map/ppermute | solution.py:23
  230.5 5.9 %collective-permute-start.6 = (f32[3,18,1,512]{3,2,1,0:T(1,128)S(1)}, f32[3,18,1,512]{3,2,1,0:T(1,128)S(1)}, u32[]{:S(2)}, u32[]{:S(2)}) collective-permute-start(f32[3,18,1,512]{3,2,1,0:T(1,128)S(1)} %get-tuple-element.51), channel_id=1, source_target_pairs={{0,1},{1,2},{2,3},{4,5},{5,6},{6,7},{8,9},{9,10},{10,11},{12,13},{... | collective-permute-start | bytes 331784 | tf_op jit(solution)/shard_map/ppermute | solution.py:21
  234.3 5.5 %collective-permute-start.7 = (f32[3,18,1,512]{3,2,1,0:T(1,128)S(1)}, f32[3,18,1,512]{3,2,1,0:T(1,128)S(1)}, u32[]{:S(2)}, u32[]{:S(2)}) collective-permute-start(f32[3,18,1,512]{3,2,1,0:T(1,128)S(1)} %get-tuple-element.52), channel_id=1, source_target_pairs={{1,0},{2,1},{3,2},{5,4},{6,5},{7,6},{9,8},{10,9},{11,10},{13,12},{... | collective-permute-start | bytes 331784 | tf_op jit(solution)/shard_map/ppermute | solution.py:23
  241.6 1.9 copy-start.3
  253.2 11.2 %copy-start.1 = (f32[6,16,16,512]{3,2,1,0:T(8,128)}, f32[6,16,16,512]{3,2,1,0:T(8,128)S(1)}, u32[]{:S(2)}) copy-start(f32[6,16,16,512]{3,2,1,0:T(8,128)S(1)} %get-tuple-element.6) | copy-start | bytes 9437188
  253.2 5.8 %collective-permute-start.8 = (f32[6,1,16,512]{3,2,1,0:T(8,128)S(1)}, f32[6,1,16,512]{3,2,1,0:T(8,128)S(1)}, u32[]{:S(2)}, u32[]{:S(2)}) collective-permute-start(f32[6,1,16,512]{3,2,1,0:T(8,128)S(1)} %get-tuple-element.45), channel_id=1, source_target_pairs={{0,4},{4,8},{8,12},{12,16},{16,20},{20,24},{24,28},{1,5},{5,9},{9,... | collective-permute-start | bytes 589832 | tf_op jit(solution)/shard_map/ppermute | solution.py:21
  256.5 7.9 %collective-permute-start.9 = (f32[6,1,16,512]{3,2,1,0:T(8,128)S(1)}, f32[6,1,16,512]{3,2,1,0:T(8,128)S(1)}, u32[]{:S(2)}, u32[]{:S(2)}) collective-permute-start(f32[6,1,16,512]{3,2,1,0:T(8,128)S(1)} %get-tuple-element.46), channel_id=1, source_target_pairs={{4,0},{8,4},{12,8},{16,12},{20,16},{24,20},{28,24},{5,1},{9,5},{13... | collective-permute-start | bytes 589832 | tf_op jit(solution)/shard_map/ppermute | solution.py:23
  264.4 7.4 %copy-start.25 = (f32[6,1,16,512]{3,2,1,0:T(8,128)}, f32[6,1,16,512]{3,2,1,0:T(8,128)S(1)}, u32[]{:S(2)}) copy-start(f32[6,1,16,512]{3,2,1,0:T(8,128)S(1)} %collective-permute-done.9) | copy-start | bytes 589828
  265.6 11.7 %collective-permute-start.10 = (f32[6,18,1,512]{3,2,1,0:T(1,128)}, f32[6,18,1,512]{3,2,1,0:T(1,128)}, u32[]{:S(2)}, u32[]{:S(2)}) collective-permute-start(f32[6,18,1,512]{3,2,1,0:T(1,128)} %get-tuple-element.30), channel_id=1, source_target_pairs={{0,1},{1,2},{2,3},{4,5},{5,6},{6,7},{8,9},{9,10},{10,11},{12,13},{... | collective-permute-start | bytes 663560 | tf_op jit(solution)/shard_map/ppermute | solution.py:21
  267.5 9.8 %collective-permute-start.11 = (f32[6,18,1,512]{3,2,1,0:T(1,128)}, f32[6,18,1,512]{3,2,1,0:T(1,128)}, u32[]{:S(2)}, u32[]{:S(2)}) collective-permute-start(f32[6,18,1,512]{3,2,1,0:T(1,128)} %get-tuple-element.31), channel_id=1, source_target_pairs={{1,0},{2,1},{3,2},{5,4},{6,5},{7,6},{9,8},{10,9},{11,10},{13,12},{... | collective-permute-start | bytes 663560 | tf_op jit(solution)/shard_map/ppermute | solution.py:23
  273.4 3.9 copy-start.2
  283.1 1.8 copy-start.5
  283.1 1.8 copy-start.13
  291.8 5.3 %copy-start.10 = (f32[16,16,512]{2,1,0:T(8,128)S(1)}, f32[16,16,512]{2,1,0:T(8,128)}, u32[]{:S(2)}) copy-start(f32[16,16,512]{2,1,0:T(8,128)} %fusion.25) | copy-start | bytes 1572868
  328.6 2.9 copy-start.12
  331.5 12.5 %copy-start.9 = (f32[8192,16]{0,1:T(8,128)S(1)}, f32[8192,16]{0,1:T(8,128)}, u32[]{:S(2)}) copy-start(f32[8192,16]{0,1:T(8,128)} %copy-done.8) | copy-start | bytes 1572868
  331.5 12.5 %copy-start.14 = (f32[2,8,16,512]{3,1,2,0:T(8,128)S(1)}, f32[2,8,16,512]{3,1,2,0:T(8,128)}, u32[]{:S(2)}) copy-start(f32[2,8,16,512]{3,1,2,0:T(8,128)} %copy.72) | copy-start | bytes 1572868
  331.5 13.4 %copy-start.16 = (f32[1,16,16,512]{3,2,1,0:T(8,128)S(1)}, f32[1,16,16,512]{3,2,1,0:T(8,128)}, u32[]{:S(2)}) copy-start(f32[1,16,16,512]{3,2,1,0:T(8,128)} %get-tuple-element.54) | copy-start | bytes 1572868
  462.5 10.7 %copy-start.6 = (f32[3,16,16,512]{3,2,1,0:T(8,128)}, f32[3,16,16,512]{3,2,1,0:T(8,128)S(1)}, u32[]{:S(2)}) copy-start(f32[3,16,16,512]{3,2,1,0:T(8,128)S(1)} %all_to_all.61) | copy-start | bytes 4718596
  462.5 5.5 %collective-permute-start.12 = (f32[3,1,16,512]{3,2,1,0:T(8,128)S(1)}, f32[3,1,16,512]{3,2,1,0:T(8,128)S(1)}, u32[]{:S(2)}, u32[]{:S(2)}) collective-permute-start(f32[3,1,16,512]{3,2,1,0:T(8,128)S(1)} %get-tuple-element.56), channel_id=1, source_target_pairs={{0,4},{4,8},{8,12},{12,16},{16,20},{20,24},{24,28},{1,5},{5,9},{9,... | collective-permute-start | bytes 294920 | tf_op jit(solution)/shard_map/ppermute | solution.py:21
  466.1 6.8 %collective-permute-start.13 = (f32[3,1,16,512]{3,2,1,0:T(8,128)S(1)}, f32[3,1,16,512]{3,2,1,0:T(8,128)S(1)}, u32[]{:S(2)}, u32[]{:S(2)}) collective-permute-start(f32[3,1,16,512]{3,2,1,0:T(8,128)S(1)} %get-tuple-element.55), channel_id=1, source_target_pairs={{4,0},{8,4},{12,8},{16,12},{20,16},{24,20},{28,24},{5,1},{9,5},{13... | collective-permute-start | bytes 294920 | tf_op jit(solution)/shard_map/ppermute | solution.py:23
  473.1 5.9 %collective-permute-start.14 = (f32[3,18,1,512]{3,2,1,0:T(1,128)S(1)}, f32[3,18,1,512]{3,2,1,0:T(1,128)S(1)}, u32[]{:S(2)}, u32[]{:S(2)}) collective-permute-start(f32[3,18,1,512]{3,2,1,0:T(1,128)S(1)} %get-tuple-element.49), channel_id=1, source_target_pairs={{0,1},{1,2},{2,3},{4,5},{5,6},{6,7},{8,9},{9,10},{10,11},{12,13},{... | collective-permute-start | bytes 331784 | tf_op jit(solution)/shard_map/ppermute | solution.py:21
  476.9 5.5 %collective-permute-start.15 = (f32[3,18,1,512]{3,2,1,0:T(1,128)S(1)}, f32[3,18,1,512]{3,2,1,0:T(1,128)S(1)}, u32[]{:S(2)}, u32[]{:S(2)}) collective-permute-start(f32[3,18,1,512]{3,2,1,0:T(1,128)S(1)} %get-tuple-element.50), channel_id=1, source_target_pairs={{1,0},{2,1},{3,2},{5,4},{6,5},{7,6},{9,8},{10,9},{11,10},{13,12},{... | collective-permute-start | bytes 331784 | tf_op jit(solution)/shard_map/ppermute | solution.py:23
  488.4 1.0 copy-start.22
  489.0 1.1 copy-start.19
  490.8 1.7 copy-start.26
  (4 other events, 4.2 us)
Sparse Core Ops, SparseCore 0:
  40.7 43.2 all-gather.4
  286.8 41.7 all-gather.6
where the time goes:
time: 505 us; the launch traced here: 499 us
  local copies, waits for them, and re-layouts  145 us (29%)
  blocking collectives  120 us (24%)
  waiting for transfers between devices  86.1 us (17%)
  other arithmetic  70.9 us (14%)
  starting transfers between devices  45.2 us (9%)
  matrix products  17.4 us (3%)
  between operations  15.1 us (3%)
    unnamed x88, local copies, waits for them, and re-layouts  65.1 us
    all_gather x2, waiting for transfers between devices, body(): piece = lax.all_gather(velocity[2], 'gy', axis=1, tiled=True)  55.9 us
    all_to_all x2, blocking collectives, damp_columns(): lax.all_to_all(velocity, 'gx', split_axis=3, concat_axis=1, tiled=True)  52.6 us
    all_to_all x2, blocking collectives, damp_columns(): return lax.all_to_all(damped, 'gx', split_axis=1, concat_axis=3, tiled=True)  48.9 us
    ppermute x8, starting transfers between devices, extended(): lax.ppermute(tail, axis, [(i, (i + 1) % count) for i in range(ends)])  26.7 us
    ppermute x8, waiting for transfers between devices, extended(): lax.ppermute(head, axis, [((i + 1) % count, i) for i in range(ends)])  26.2 us
    all_gather x2, blocking collectives, body(): all_force = lax.all_gather(force, 'gy', axis=1, tiled=True)  18.4 us
    ppermute x8, starting transfers between devices, extended(): lax.ppermute(head, axis, [((i + 1) % count, i) for i in range(ends)])  18.2 us
  transfers between devices with their start and end apart: 18, of which 12 were waited for; matrix products, arithmetic and copies ran while one was open for 8% of the time, Pallas kernels for 0%

commit v1 on v0

--- a/solution.py
+++ b/solution.py
@@ -103,7 +103,10 @@
 
 
 def damp_columns(velocity, inverse):
-    pencils = lax.all_to_all(velocity, "gx", split_axis=3, concat_axis=1, tiled=True)
+    pencils = jnp.concatenate(
+        lax.all_to_all(jnp.stack(jnp.split(velocity, lax.axis_size("gx"), axis=3)), "gx", 0, 0),
+        axis=1,
+    )
     shape = pencils.shape
     flat = pencils.reshape(shape[0], shape[1], shape[2] * shape[3])
     damped = jnp.einsum("zk,fkm->fzm", inverse, flat, precision=lax.Precision.HIGHEST).reshape(

time: 505 us -> 469 us (0.929)
  local copies, waits for them, and re-layouts: 145 us -> 108 us
    all_to_all x3 -> x1, local copies, waits for them, and re-layouts: 16.8 us -> 0.52 us  [damp_columns(): lax.all_to_all(jnp.stack(jnp.split(velocity, lax.axis_size('gx'), axis=3)...]
    unnamed x88 -> x102, local copies, waits for them, and re-layouts: 65.1 us -> 54.3 us
    another operation x2 -> x4, local copies, waits for them, and re-layouts: 17.6 us -> 7.57 us  [the longest x2 5.74 us: damp_columns(): flat = pencils.reshape(shape[0], shape[1], shape[2] * shape[3])]
where the time goes in v1:
time: 469 us; the launch traced here: 463 us
  blocking collectives  120 us (26%)
  local copies, waits for them, and re-layouts  108 us (23%)
  waiting for transfers between devices  85.7 us (18%)
  other arithmetic  74.2 us (16%)
  starting transfers between devices  45.7 us (10%)
  between operations  15.1 us (3%)
  matrix products  14.6 us (3%)
    all_gather x2, waiting for transfers between devices, body(): piece = lax.all_gather(velocity[2], 'gy', axis=1, tiled=True)  55.6 us
    unnamed x102, local copies, waits for them, and re-layouts  54.3 us
    all_to_all x2, blocking collectives, damp_columns(): lax.all_to_all(jnp.stack(jnp.split(velocity, lax.axis_size('gx'), axis=3)...  52.2 us
    all_to_all x2, blocking collectives, damp_columns(): return lax.all_to_all(damped, 'gx', split_axis=1, concat_axis=3, tiled=True)  49.6 us
    ppermute x8, starting transfers between devices, extended(): lax.ppermute(tail, axis, [(i, (i + 1) % count) for i in range(ends)])  26.7 us
    ppermute x8, waiting for transfers between devices, extended(): lax.ppermute(head, axis, [((i + 1) % count, i) for i in range(ends)])  26 us
    all_gather x2, blocking collectives, body(): all_force = lax.all_gather(force, 'gy', axis=1, tiled=True)  18.6 us
    ppermute x8, starting transfers between devices, extended(): lax.ppermute(head, axis, [((i + 1) % count, i) for i in range(ends)])  18.4 us
  transfers between devices with their start and end apart: 18, of which 12 were waited for; matrix products, arithmetic and copies ran while one was open for 8% of the time, Pallas kernels for 0%

profile of v1, /device:TPU:11, one launch (start us, length us, event | category | flops | bytes accessed | tf_op | source)
XLA Modules:
  0.0 463.2 jit_solution(16718585672030012925)
XLA Ops:
  8.3 3.7 collective-permute-start
  16.9 3.0 collective-permute-done.1
  20.3 3.2 collective-permute-start.2
  25.6 2.9 collective-permute-done.2
  28.5 3.2 collective-permute-done.3
  31.7 4.2 select_maximum_fusion.4
  41.2 2.9 convert_reduce_fusion.1
  48.2 4.9 %fusion.58 = (f32[1,16,16,512]{3,2,1,0:T(8,128)}, f32[1,16,16,512]{3,2,1,0:T(8,128)}) fusion(f32[18,18,514]{2,1,0:T(8,128)S(1)} %get-tuple-element.27, f32[18,18,514]{2,1,0:T(8,128)S(1)} %copy-done.7, f32[18,18,514]{2,1,0:T(8,128)} %get-tuple-element.24, f32[3,16,16,512]{3,2,1,0:T(8,128)} %param.11, f32[16,16,512]{2,1,0:T(8,128)S(1)} %copy-done.4, ...), kind=kLoop, calls=%fused_computation.133 | loop fusion | flops 1966080 | bytes 8388608 | tf_op jit(solution)/shard_map/stack | solution.py:59
  53.2 30.8 %all-gather.5.cloned.1.call-done = f32[16,64,512]{2,1,0:T(8,128)} async-done(((f32[16,16,512]{2,1,0:T(8,128)}), f32[16,64,512]{2,1,0:T(8,128)}) %all-gather.5.cloned.1.call-update) | async-done | bytes 2097168 | tf_op jit(solution)/shard_map/all_gather | solution.py:144
  84.0 2.9 copy.66
  89.5 9.2 %all-gather = f32[4,4,16]{2,1,0:T(4,128)S(1)} all-gather(f32[1,4,16]{2,1,0:T(4,128)S(1)} %bitcast.268), channel_id=1, replica_groups=mesh['gx'=8,'gy'=4] {'gy'}, dimensions={0}, use_global_device_ids=true | all-gather | bytes 1280 | tf_op jit(solution)/shard_map/all_gather | solution.py:155
  106.8 3.8 reshape.87
  110.6 26.2 %all_to_all.46 = f32[8,1,49152]{2,1,0:T(1,128)S(1)} all-to-all(f32[8,1,49152]{2,1,0:T(1,128)S(1)} %reshape.87), channel_id=1, replica_groups=mesh['gx'=8,'gy'=4] {'gx'}, dimensions={0} | all-to-all | bytes 3145728 | tf_op jit(solution)/shard_map/all_to_all | solution.py:107
  137.3 6.1 %reduce = f32[8,49152]{1,0:T(8,128)} reduce(f32[8,1,49152]{2,1,0:T(1,128)S(1)} %all_to_all.46, f32[]{:T(128)} %broadcast.158), dimensions={1}, to_apply=%all_to_all.32.reduce_sub_computation | reduce | bytes 3145732 | tf_op jit(solution)/shard_map/all_to_all | solution.py:107
  148.0 2.9 reshape_reshape.6
  150.9 3.8 fusion.81
  157.0 3.0 reshape.89
  160.0 24.7 %all_to_all.47 = f32[8,1,49152]{2,1,0:T(1,128)S(1)} all-to-all(f32[8,1,49152]{2,1,0:T(1,128)} %reshape.89), channel_id=1, replica_groups=mesh['gx'=8,'gy'=4] {'gx'}, dimensions={0} | all-to-all | bytes 3145728 | tf_op jit(solution)/shard_map/all_to_all | solution.py:115
  184.7 6.1 %reduce.1 = f32[8,49152]{1,0:T(8,128)} reduce(f32[8,1,49152]{2,1,0:T(1,128)S(1)} %all_to_all.47, f32[]{:T(128)} %broadcast.158), dimensions={1}, to_apply=%all_to_all.33.reduce_sub_computation | reduce | bytes 3145732 | tf_op jit(solution)/shard_map/all_to_all | solution.py:115
  193.5 3.5 copy.53
  197.0 3.8 all_to_all.36
  201.7 3.5 collective-permute-start.4
  208.9 3.3 collective-permute-done.5
  212.4 3.8 collective-permute-start.6
  218.6 3.1 collective-permute-done.7
  235.3 3.2 collective-permute-start.8
  241.1 5.3 %collective-permute-done.9 = f32[6,1,16,512]{3,2,1,0:T(8,128)S(1)} collective-permute-done((f32[6,1,16,512]{3,2,1,0:T(8,128)S(1)}, f32[6,1,16,512]{3,2,1,0:T(8,128)S(1)}, u32[]{:S(2)}, u32[]{:S(2)}) %collective-permute-start.9) | collective-permute-done | bytes 196640 | tf_op jit(solution)/shard_map/ppermute | solution.py:23
  249.6 4.2 collective-permute-start.11
  259.3 5.8 %select_maximum_fusion = f32[6,18,18,514]{3,2,1,0:T(8,128)S(1)} fusion(f32[6,18,1,512]{3,2,1,0:T(1,128)} %collective-permute-done.11, f32[6,18,1,512]{3,2,1,0:T(1,128)} %collective-permute-done.10, f32[6,1,16,512]{3,2,1,0:T(8,128)} %copy-done.25, f32[6,16,16,512]{3,2,1,0:T(8,128)S(1)} %copy-done.2, f32[6,1,16,512]{3,2,1,0:T(8,128)S(1)} %collective-permute-done.8), kind=kLoop, calls=%fused_computation.9 | loop fusion | flops 11990592 | bytes 7978176 | tf_op jit(solution)/shard_map/concatenate | solution.py:19
  273.9 2.9 copy.54
  280.2 5.6 %fusion.35 = (f32[1,16,16,512]{3,2,1,0:T(8,128)S(1)}, f32[1,16,16,512]{3,2,1,0:T(8,128)}) fusion(f32[16,16,512]{2,1,0:T(8,128)} %squeeze.117, f32[18,18,514]{2,1,0:T(8,128)S(1)} %get-tuple-element.21, f32[18,18,514]{2,1,0:T(8,128)} %get-tuple-element.22, f32[18,18,514]{2,1,0:T(8,128)} %get-tuple-element.18, f32[16,16,512]{2,1,0:T(8,128)S(1)} %copy-done.5, ...), kind=kLoop, calls=%fused_computation.92 | loop fusion | flops 1966080 | bytes 8388608 | tf_op jit(solution)/shard_map/stack | solution.py:59
  285.8 24.8 %all-gather.7.cloned.1.call-done = f32[16,64,512]{2,1,0:T(8,128)} async-done(((f32[16,16,512]{2,1,0:T(8,128)}), f32[16,64,512]{2,1,0:T(8,128)}) %all-gather.7.cloned.1.call-update) | async-done | bytes 2097168 | tf_op jit(solution)/shard_map/all_gather | solution.py:144
  310.6 2.9 copy.69
  313.5 3.3 multiply_subtract_fusion
  316.8 9.4 %all-gather.1 = f32[4,4,16]{2,1,0:T(4,128)S(1)} all-gather(f32[1,4,16]{2,1,0:T(4,128)S(1)} %bitcast.269), channel_id=1, replica_groups=mesh['gx'=8,'gy'=4] {'gy'}, dimensions={0}, use_global_device_ids=true | all-gather | bytes 1280 | tf_op jit(solution)/shard_map/all_gather | solution.py:155
  334.2 3.8 reshape.91
  338.0 26.0 %all_to_all.48 = f32[8,1,49152]{2,1,0:T(1,128)S(1)} all-to-all(f32[8,1,49152]{2,1,0:T(1,128)S(1)} %reshape.91), channel_id=1, replica_groups=mesh['gx'=8,'gy'=4] {'gx'}, dimensions={0} | all-to-all | bytes 3145728 | tf_op jit(solution)/shard_map/all_to_all | solution.py:107
  364.0 6.1 %reduce.2 = f32[8,49152]{1,0:T(8,128)} reduce(f32[8,1,49152]{2,1,0:T(1,128)S(1)} %all_to_all.48, f32[]{:T(128)} %broadcast.158), dimensions={1}, to_apply=%all_to_all.37.reduce_sub_computation | reduce | bytes 3145732 | tf_op jit(solution)/shard_map/all_to_all | solution.py:107
  374.8 2.9 reshape_reshape.7
  377.6 3.8 fusion.79
  383.7 3.0 reshape.93
  386.7 24.9 %all_to_all.49 = f32[8,1,49152]{2,1,0:T(1,128)S(1)} all-to-all(f32[8,1,49152]{2,1,0:T(1,128)} %reshape.93), channel_id=1, replica_groups=mesh['gx'=8,'gy'=4] {'gx'}, dimensions={0} | all-to-all | bytes 3145728 | tf_op jit(solution)/shard_map/all_to_all | solution.py:115
  411.6 6.1 %reduce.3 = f32[8,49152]{1,0:T(8,128)} reduce(f32[8,1,49152]{2,1,0:T(1,128)S(1)} %all_to_all.49, f32[]{:T(128)} %broadcast.158), dimensions={1}, to_apply=%all_to_all.38.reduce_sub_computation | reduce | bytes 3145732 | tf_op jit(solution)/shard_map/all_to_all | solution.py:115
  420.4 3.5 copy.60
  426.8 3.5 collective-permute-start.12
  432.4 4.7 %collective-permute-done.13 = f32[3,1,16,512]{3,2,1,0:T(8,128)S(1)} collective-permute-done((f32[3,1,16,512]{3,2,1,0:T(8,128)S(1)}, f32[3,1,16,512]{3,2,1,0:T(8,128)S(1)}, u32[]{:S(2)}, u32[]{:S(2)}) %collective-permute-start.13) | collective-permute-done | bytes 98336 | tf_op jit(solution)/shard_map/ppermute | solution.py:23
  437.4 3.8 collective-permute-start.14
  443.3 3.4 collective-permute-done.15
  (172 shorter events, 116.7 us)
Async XLA Ops:
  7.2 143.7 %copy-start = (f32[128,128]{1,0:T(8,128)S(1)}, f32[128,128]{1,0:T(8,128)}, u32[]{:S(2)}) copy-start(f32[128,128]{1,0:T(8,128)} %param.21) | copy-start | bytes 196612
  7.2 76.8 %all-gather.5.cloned.1.call-start = ((), (), s32[]{:S(2)}) async-start(), calls=%async_computation.4 | async-start | bytes 2621440 | tf_op jit(solution)/shard_map/all_gather | solution.py:144
  8.3 6.3 %collective-permute-start = (f32[6,1,16,512]{3,2,1,0:T(8,128)S(1)}, f32[6,1,16,512]{3,2,1,0:T(8,128)S(1)}, u32[]{:S(2)}, u32[]{:S(2)}) collective-permute-start(f32[6,1,16,512]{3,2,1,0:T(8,128)S(1)} %get-tuple-element.48), channel_id=1, source_target_pairs={{0,4},{4,8},{8,12},{12,16},{16,20},{20,24},{24,28},{1,5},{5,9},{9,... | collective-permute-start | bytes 589832 | tf_op jit(solution)/shard_map/ppermute | solution.py:21
  12.0 7.9 %collective-permute-start.1 = (f32[6,1,16,512]{3,2,1,0:T(8,128)S(1)}, f32[6,1,16,512]{3,2,1,0:T(8,128)S(1)}, u32[]{:S(2)}, u32[]{:S(2)}) collective-permute-start(f32[6,1,16,512]{3,2,1,0:T(8,128)S(1)} %get-tuple-element.47), channel_id=1, source_target_pairs={{4,0},{8,4},{12,8},{16,12},{20,16},{24,20},{28,24},{5,1},{9,5},{13... | collective-permute-start | bytes 589832 | tf_op jit(solution)/shard_map/ppermute | solution.py:23
  20.3 8.2 %collective-permute-start.2 = (f32[6,18,1,512]{3,2,1,0:T(1,128)S(1)}, f32[6,18,1,512]{3,2,1,0:T(1,128)S(1)}, u32[]{:S(2)}, u32[]{:S(2)}) collective-permute-start(f32[6,18,1,512]{3,2,1,0:T(1,128)S(1)} %get-tuple-element.32), channel_id=1, source_target_pairs={{0,1},{1,2},{2,3},{4,5},{5,6},{6,7},{8,9},{9,10},{10,11},{12,13},{... | collective-permute-start | bytes 663560 | tf_op jit(solution)/shard_map/ppermute | solution.py:21
  23.5 8.2 %collective-permute-start.3 = (f32[6,18,1,512]{3,2,1,0:T(1,128)S(1)}, f32[6,18,1,512]{3,2,1,0:T(1,128)S(1)}, u32[]{:S(2)}, u32[]{:S(2)}) collective-permute-start(f32[6,18,1,512]{3,2,1,0:T(1,128)S(1)} %get-tuple-element.33), channel_id=1, source_target_pairs={{1,0},{2,1},{3,2},{5,4},{6,5},{7,6},{9,8},{10,9},{11,10},{13,12},{... | collective-permute-start | bytes 663560 | tf_op jit(solution)/shard_map/ppermute | solution.py:23
  35.9 1.8 copy-start.4
  37.8 3.4 copy-start.27
  40.6 270.0 %all-gather.7.cloned.1.call-start = ((), (), s32[]{:S(2)}) async-start(), calls=%async_computation.5 | async-start | bytes 2621440 | tf_op jit(solution)/shard_map/all_gather | solution.py:144
  41.2 7.0 %copy-start.7 = (f32[18,18,514]{2,1,0:T(8,128)S(1)}, f32[18,18,514]{2,1,0:T(8,128)}, u32[]{:S(2)}) copy-start(f32[18,18,514]{2,1,0:T(8,128)} %get-tuple-element.28) | copy-start | bytes 1998436
  45.8 52.9 %copy-start.8 = (f32[8192,16]{0,1:T(8,128)}, f32[8192,16]{0,1:T(8,128)S(1)}, u32[]{:S(2)}) copy-start(f32[8192,16]{0,1:T(8,128)S(1)} %convert_reduce_fusion) | copy-start | bytes 1572868
  53.1 33.7 %copy-start.11 = (f32[32768,4]{0,1:T(4,128)S(1)}, f32[32768,4]{0,1:T(4,128)}, u32[]{:S(2)}) copy-start(f32[32768,4]{0,1:T(4,128)} %convert_reduce_fusion.1) | copy-start | bytes 1572868
  53.2 33.7 %copy-start.28 = (f32[16,4]{0,1:T(4,128)S(1)}, f32[16,4]{0,1:T(4,128)}, u32[]{:S(2)}) copy-start(f32[16,4]{0,1:T(4,128)} %param.13) | copy-start | bytes 772
  53.2 33.7 %copy-start.29 = (f32[4]{0:T(128)S(1)}, f32[4]{0:T(128)}, u32[]{:S(2)}) copy-start(f32[4]{0:T(128)} %param.19) | copy-start | bytes 52
  84.0 14.7 %copy-start.15 = (f32[2,8,16,512]{3,1,2,0:T(8,128)S(1)}, f32[2,8,16,512]{3,1,2,0:T(8,128)}, u32[]{:S(2)}) copy-start(f32[2,8,16,512]{3,1,2,0:T(8,128)} %copy.65) | copy-start | bytes 1572868
  86.8 12.8 %copy-start.17 = (f32[1,16,16,512]{3,2,1,0:T(8,128)S(1)}, f32[1,16,16,512]{3,2,1,0:T(8,128)}, u32[]{:S(2)}) copy-start(f32[1,16,16,512]{3,2,1,0:T(8,128)} %get-tuple-element.40) | copy-start | bytes 1572868
  86.9 12.8 %copy-start.18 = (f32[1,16,16,512]{3,2,1,0:T(8,128)S(1)}, f32[1,16,16,512]{3,2,1,0:T(8,128)}, u32[]{:S(2)}) copy-start(f32[1,16,16,512]{3,2,1,0:T(8,128)} %get-tuple-element.41) | copy-start | bytes 1572868
  197.0 8.3 %copy-start.30 = (f32[8]{0:T(128)S(1)}, f32[8]{0:T(128)}, u32[]{:S(2)}) copy-start(f32[8]{0:T(128)} %param.18) | copy-start | bytes 100
  197.0 8.3 %copy-start.31 = (s32[16]{0:T(128)S(1)}, s32[16]{0:T(128)}, u32[]{:S(2)}) copy-start(s32[16]{0:T(128)} %param.15) | copy-start | bytes 196
  197.0 8.3 %copy-start.32 = (f32[8]{0:T(128)S(1)}, f32[8]{0:T(128)}, u32[]{:S(2)}) copy-start(f32[8]{0:T(128)} %param.17) | copy-start | bytes 100
  197.0 8.3 %copy-start.33 = (f32[8]{0:T(128)S(1)}, f32[8]{0:T(128)}, u32[]{:S(2)}) copy-start(f32[8]{0:T(128)} %param.16) | copy-start | bytes 100
  201.7 5.6 %collective-permute-start.4 = (f32[3,1,16,512]{3,2,1,0:T(8,128)S(1)}, f32[3,1,16,512]{3,2,1,0:T(8,128)S(1)}, u32[]{:S(2)}, u32[]{:S(2)}) collective-permute-start(f32[3,1,16,512]{3,2,1,0:T(8,128)S(1)} %get-tuple-element.58), channel_id=1, source_target_pairs={{0,4},{4,8},{8,12},{12,16},{16,20},{20,24},{24,28},{1,5},{5,9},{9,... | collective-permute-start | bytes 294920 | tf_op jit(solution)/shard_map/ppermute | solution.py:21
  205.4 6.8 %collective-permute-start.5 = (f32[3,1,16,512]{3,2,1,0:T(8,128)S(1)}, f32[3,1,16,512]{3,2,1,0:T(8,128)S(1)}, u32[]{:S(2)}, u32[]{:S(2)}) collective-permute-start(f32[3,1,16,512]{3,2,1,0:T(8,128)S(1)} %get-tuple-element.57), channel_id=1, source_target_pairs={{4,0},{8,4},{12,8},{16,12},{20,16},{24,20},{28,24},{5,1},{9,5},{13... | collective-permute-start | bytes 294920 | tf_op jit(solution)/shard_map/ppermute | solution.py:23
  212.4 6.1 %collective-permute-start.6 = (f32[3,18,1,512]{3,2,1,0:T(1,128)S(1)}, f32[3,18,1,512]{3,2,1,0:T(1,128)S(1)}, u32[]{:S(2)}, u32[]{:S(2)}) collective-permute-start(f32[3,18,1,512]{3,2,1,0:T(1,128)S(1)} %get-tuple-element.51), channel_id=1, source_target_pairs={{0,1},{1,2},{2,3},{4,5},{5,6},{6,7},{8,9},{9,10},{10,11},{12,13},{... | collective-permute-start | bytes 331784 | tf_op jit(solution)/shard_map/ppermute | solution.py:21
  216.2 5.5 %collective-permute-start.7 = (f32[3,18,1,512]{3,2,1,0:T(1,128)S(1)}, f32[3,18,1,512]{3,2,1,0:T(1,128)S(1)}, u32[]{:S(2)}, u32[]{:S(2)}) collective-permute-start(f32[3,18,1,512]{3,2,1,0:T(1,128)S(1)} %get-tuple-element.52), channel_id=1, source_target_pairs={{1,0},{2,1},{3,2},{5,4},{6,5},{7,6},{9,8},{10,9},{11,10},{13,12},{... | collective-permute-start | bytes 331784 | tf_op jit(solution)/shard_map/ppermute | solution.py:23
  223.5 1.9 copy-start.3
  235.2 11.2 %copy-start.1 = (f32[6,16,16,512]{3,2,1,0:T(8,128)}, f32[6,16,16,512]{3,2,1,0:T(8,128)S(1)}, u32[]{:S(2)}) copy-start(f32[6,16,16,512]{3,2,1,0:T(8,128)S(1)} %get-tuple-element.6) | copy-start | bytes 9437188
  235.3 5.8 %collective-permute-start.8 = (f32[6,1,16,512]{3,2,1,0:T(8,128)S(1)}, f32[6,1,16,512]{3,2,1,0:T(8,128)S(1)}, u32[]{:S(2)}, u32[]{:S(2)}) collective-permute-start(f32[6,1,16,512]{3,2,1,0:T(8,128)S(1)} %get-tuple-element.45), channel_id=1, source_target_pairs={{0,4},{4,8},{8,12},{12,16},{16,20},{20,24},{24,28},{1,5},{5,9},{9,... | collective-permute-start | bytes 589832 | tf_op jit(solution)/shard_map/ppermute | solution.py:21
  238.5 7.9 %collective-permute-start.9 = (f32[6,1,16,512]{3,2,1,0:T(8,128)S(1)}, f32[6,1,16,512]{3,2,1,0:T(8,128)S(1)}, u32[]{:S(2)}, u32[]{:S(2)}) collective-permute-start(f32[6,1,16,512]{3,2,1,0:T(8,128)S(1)} %get-tuple-element.46), channel_id=1, source_target_pairs={{4,0},{8,4},{12,8},{16,12},{20,16},{24,20},{28,24},{5,1},{9,5},{13... | collective-permute-start | bytes 589832 | tf_op jit(solution)/shard_map/ppermute | solution.py:23
  246.4 9.0 %copy-start.25 = (f32[6,1,16,512]{3,2,1,0:T(8,128)}, f32[6,1,16,512]{3,2,1,0:T(8,128)S(1)}, u32[]{:S(2)}) copy-start(f32[6,1,16,512]{3,2,1,0:T(8,128)S(1)} %collective-permute-done.9) | copy-start | bytes 589828
  247.6 11.7 %collective-permute-start.10 = (f32[6,18,1,512]{3,2,1,0:T(1,128)}, f32[6,18,1,512]{3,2,1,0:T(1,128)}, u32[]{:S(2)}, u32[]{:S(2)}) collective-permute-start(f32[6,18,1,512]{3,2,1,0:T(1,128)} %get-tuple-element.30), channel_id=1, source_target_pairs={{0,1},{1,2},{2,3},{4,5},{5,6},{6,7},{8,9},{9,10},{10,11},{12,13},{... | collective-permute-start | bytes 663560 | tf_op jit(solution)/shard_map/ppermute | solution.py:21
  249.6 9.8 %collective-permute-start.11 = (f32[6,18,1,512]{3,2,1,0:T(1,128)}, f32[6,18,1,512]{3,2,1,0:T(1,128)}, u32[]{:S(2)}, u32[]{:S(2)}) collective-permute-start(f32[6,18,1,512]{3,2,1,0:T(1,128)} %get-tuple-element.31), channel_id=1, source_target_pairs={{1,0},{2,1},{3,2},{5,4},{6,5},{7,6},{9,8},{10,9},{11,10},{13,12},{... | collective-permute-start | bytes 663560 | tf_op jit(solution)/shard_map/ppermute | solution.py:23
  255.4 3.9 copy-start.2
  265.1 1.8 copy-start.5
  265.1 1.8 copy-start.13
  271.5 7.5 %copy-start.10 = (f32[16,16,512]{2,1,0:T(8,128)S(1)}, f32[16,16,512]{2,1,0:T(8,128)}, u32[]{:S(2)}) copy-start(f32[16,16,512]{2,1,0:T(8,128)} %fusion.25) | copy-start | bytes 1572868
  285.8 27.7 %copy-start.12 = (f32[32768,4]{0,1:T(4,128)S(1)}, f32[32768,4]{0,1:T(4,128)}, u32[]{:S(2)}) copy-start(f32[32768,4]{0,1:T(4,128)} %convert_reduce_fusion.1) | copy-start | bytes 1572868
  310.6 15.6 %copy-start.9 = (f32[8192,16]{0,1:T(8,128)S(1)}, f32[8192,16]{0,1:T(8,128)}, u32[]{:S(2)}) copy-start(f32[8192,16]{0,1:T(8,128)} %copy-done.8) | copy-start | bytes 1572868
  310.6 15.6 %copy-start.14 = (f32[2,8,16,512]{3,1,2,0:T(8,128)S(1)}, f32[2,8,16,512]{3,1,2,0:T(8,128)}, u32[]{:S(2)}) copy-start(f32[2,8,16,512]{3,1,2,0:T(8,128)} %copy.68) | copy-start | bytes 1572868
  313.5 13.6 %copy-start.16 = (f32[1,16,16,512]{3,2,1,0:T(8,128)S(1)}, f32[1,16,16,512]{3,2,1,0:T(8,128)}, u32[]{:S(2)}) copy-start(f32[1,16,16,512]{3,2,1,0:T(8,128)} %get-tuple-element.54) | copy-start | bytes 1572868
  426.7 21.7 %copy-start.6 = (f32[3,16,16,512]{3,2,1,0:T(8,128)}, f32[3,16,16,512]{3,2,1,0:T(8,128)S(1)}, u32[]{:S(2)}) copy-start(f32[3,16,16,512]{3,2,1,0:T(8,128)S(1)} %all_to_all.41) | copy-start | bytes 4718596
  426.8 5.5 %collective-permute-start.12 = (f32[3,1,16,512]{3,2,1,0:T(8,128)S(1)}, f32[3,1,16,512]{3,2,1,0:T(8,128)S(1)}, u32[]{:S(2)}, u32[]{:S(2)}) collective-permute-start(f32[3,1,16,512]{3,2,1,0:T(8,128)S(1)} %get-tuple-element.56), channel_id=1, source_target_pairs={{0,4},{4,8},{8,12},{12,16},{16,20},{20,24},{24,28},{1,5},{5,9},{9,... | collective-permute-start | bytes 294920 | tf_op jit(solution)/shard_map/ppermute | solution.py:21
  430.3 6.8 %collective-permute-start.13 = (f32[3,1,16,512]{3,2,1,0:T(8,128)S(1)}, f32[3,1,16,512]{3,2,1,0:T(8,128)S(1)}, u32[]{:S(2)}, u32[]{:S(2)}) collective-permute-start(f32[3,1,16,512]{3,2,1,0:T(8,128)S(1)} %get-tuple-element.55), channel_id=1, source_target_pairs={{4,0},{8,4},{12,8},{16,12},{20,16},{24,20},{28,24},{5,1},{9,5},{13... | collective-permute-start | bytes 294920 | tf_op jit(solution)/shard_map/ppermute | solution.py:23
  437.4 5.9 %collective-permute-start.14 = (f32[3,18,1,512]{3,2,1,0:T(1,128)S(1)}, f32[3,18,1,512]{3,2,1,0:T(1,128)S(1)}, u32[]{:S(2)}, u32[]{:S(2)}) collective-permute-start(f32[3,18,1,512]{3,2,1,0:T(1,128)S(1)} %get-tuple-element.49), channel_id=1, source_target_pairs={{0,1},{1,2},{2,3},{4,5},{5,6},{6,7},{8,9},{9,10},{10,11},{12,13},{... | collective-permute-start | bytes 331784 | tf_op jit(solution)/shard_map/ppermute | solution.py:21
  441.2 5.5 %collective-permute-start.15 = (f32[3,18,1,512]{3,2,1,0:T(1,128)S(1)}, f32[3,18,1,512]{3,2,1,0:T(1,128)S(1)}, u32[]{:S(2)}, u32[]{:S(2)}) collective-permute-start(f32[3,18,1,512]{3,2,1,0:T(1,128)S(1)} %get-tuple-element.50), channel_id=1, source_target_pairs={{1,0},{2,1},{3,2},{5,4},{6,5},{7,6},{9,8},{10,9},{11,10},{13,12},{... | collective-permute-start | bytes 331784 | tf_op jit(solution)/shard_map/ppermute | solution.py:23
  448.7 1.8 copy-start.24
  451.5 1.7 copy-start.22
  454.5 1.7 copy-start.26
  (4 other events, 4.4 us)
Sparse Core Ops, SparseCore 0:
  40.7 43.2 all-gather.4
  268.8 41.7 all-gather.6
